TPU v7x, 256 devices: a whole 4x4x8 slice. The times are simulated.
256 devices in a mesh: section: 8 (over z_hi, x), tp: 32 (over z_lo, y, core).
Axes of the slice: x: 4, y: 4, z: 8 (z_hi: 2, z_lo: 4; z = z_hi * 4 + z_lo), core: 2. Of those that a mesh axis runs over, the one named last changes fastest.
Arguments:
- fresh_in: bfloat16 [128, 12288], P(None, 'tp'), may hold values from -25 to 25
- fwd_in: bfloat16 [8, 128, 12288], P('section', None, 'tp'), may hold values from -25 to 25
- fresh_cot: bfloat16 [128, 12288], P(None, 'tp'), may hold values from -7 to 7
- cot_in: bfloat16 [8, 128, 12288], P('section', None, 'tp'), may hold values from -7 to 7
- stash_in: bfloat16 [8, 2, 128, 12288], P('section', None, None, 'tp'), may hold values from -25 to 25
- weight: bfloat16 [8, 12288, 12288], P('section', None, 'tp'), may hold values from -0.0546875 to 0.0546875
- gain: float32 [8, 12288], P('section'), may hold values from 0.25 to 1.75
Outputs:
- first_out: bfloat16 [8, 128, 12288], P('section', None, 'tp')
- second_out: bfloat16 [8, 128, 12288], P('section', None, 'tp')
- first_grad: bfloat16 [8, 128, 12288], P('section', None, 'tp')
- second_grad: bfloat16 [8, 128, 12288], P('section', None, 'tp')
- stash_out: bfloat16 [8, 2, 128, 12288], P('section', None, None, 'tp')
All inputs are finite; a program needn't handle non-finite values.
Results may differ from a plain program's by a relative error of at most 0.019.
Values may be sent and summed in bfloat16 or wider, within the bound.
A program may use at most 64 MiB of HBM per device.

v0:
```python
import jax
import jax.numpy as jnp
from jax import lax
from jax.sharding import PartitionSpec as P

EPS = 1e-05
GCOEF = 0.7978845608028654


def from_partner(value, axis, distance):
    mask = 2**distance
    pairs = [(source, source ^ mask) for source in range(lax.axis_size(axis))]
    return lax.ppermute(value, axis, pairs)


def from_behind(block, axis, distance):
    devices = range(lax.axis_size(axis))
    route = [(i - distance, i) for i in devices if i - distance in devices]
    return lax.ppermute(block, axis, route)


def gelu_value(h):
    return 0.5 * h * (1.0 + jnp.tanh(GCOEF * (h + 0.044715 * h * h * h)))


def gelu_slope(h):
    tval = jnp.tanh(GCOEF * (h + 0.044715 * h * h * h))
    return 0.5 * (1.0 + tval) + 0.5 * h * (1.0 - tval * tval) * GCOEF * (
        1.0 + 3.0 * 0.044715 * h * h
    )


def layer_parts(full_rows, w_cols, g_full):
    xf = full_rows.astype(jnp.float32)
    radius = jnp.sqrt(jnp.mean(xf * xf, axis=-1, keepdims=True) + EPS)
    normed = (g_full[None, :] * xf / radius).astype(jnp.bfloat16)
    hidden = jnp.dot(normed, w_cols, preferred_element_type=jnp.float32)
    return (radius, hidden)


def forward(full_rows, own_rows, w_cols, g_full):
    radius, hidden = layer_parts(full_rows, w_cols, g_full)
    return (own_rows.astype(jnp.float32) + gelu_value(hidden)).astype(jnp.bfloat16)


def backward(full_rows, own_rows, cot, w_cols, g_full, g_local):
    radius, hidden = layer_parts(full_rows, w_cols, g_full)
    upstream = (cot.astype(jnp.float32) * gelu_slope(hidden)).astype(jnp.bfloat16)
    partial_sum = lax.dot_general(
        upstream, w_cols, (((1,), (1,)), ((), ())), preferred_element_type=jnp.float32
    )
    dnorm = lax.psum_scatter(
        partial_sum.astype(jnp.bfloat16), "tp", scatter_dimension=1, tiled=True
    ).astype(jnp.float32)
    own_f = own_rows.astype(jnp.float32)
    inner = lax.psum(jnp.sum(dnorm * g_local[None, :] * own_f, axis=-1, keepdims=True), "tp")
    width = g_full.shape[0]
    grad = (
        cot.astype(jnp.float32)
        + g_local[None, :] * dnorm / radius
        - own_f * inner / (width * radius**3)
    )
    return grad.astype(jnp.bfloat16)


def evict_single(block):
    for bit in range(lax.axis_size("section").bit_length() - 1):
        block = from_partner(block, "section", bit)
    return block


def gather_rows(part_rows):
    return lax.all_gather(part_rows, "tp", axis=1, tiled=True)


def shards(fresh_in, fwd_in, fresh_cot, cot_in, stash_in, weight, gain):
    local_width = fwd_in.shape[-1]
    rank = lax.axis_index("tp")
    section_now = lax.axis_index("section")
    last_section = lax.axis_size("section") - 1
    w_cols = weight[0]
    g_full = gain[0]
    g_local = lax.dynamic_slice_in_dim(g_full, rank * local_width, local_width)
    first_x = fwd_in[0]
    held = stash_in[0]
    for bit in range(lax.axis_size("section").bit_length() - 1):
        held = from_partner(held, "section", bit)
    saved_one = held[0]
    saved_two = held[1]
    full_first = gather_rows(first_x)
    full_saved_one = gather_rows(saved_one)
    first_out = forward(full_first, first_x, w_cols, g_full)
    sent_first = evict_single(first_x)
    first_grad = backward(full_saved_one, saved_one, cot_in[0], w_cols, g_full, g_local)
    arrived = from_behind(first_out, "section", 1)
    second_x = jnp.where(section_now == 0, fresh_in, arrived)
    grad_arrived = from_behind(first_grad, "section", -1)
    second_cot = jnp.where(section_now == last_section, fresh_cot, grad_arrived)
    full_second = gather_rows(second_x)
    full_saved_two = gather_rows(saved_two)
    second_out = forward(full_second, second_x, w_cols, g_full)
    sent_second = evict_single(second_x)
    stash_block = jnp.stack([sent_first, sent_second])
    second_grad = backward(full_saved_two, saved_two, second_cot, w_cols, g_full, g_local)
    return (
        first_out[None],
        second_out[None],
        first_grad[None],
        second_grad[None],
        stash_block[None],
    )


def solution(mesh):
    return jax.shard_map(
        shards,
        mesh=mesh,
        in_specs=(
            P(None, "tp"),
            P("section", None, "tp"),
            P(None, "tp"),
            P("section", None, "tp"),
            P("section", None, None, "tp"),
            P("section", None, "tp"),
            P("section", None),
        ),
        out_specs=(
            P("section", None, "tp"),
            P("section", None, "tp"),
            P("section", None, "tp"),
            P("section", None, "tp"),
            P("section", None, None, "tp"),
        ),
        check_vma=False,
    )
```

profile of v0, /device:TPU:1, one launch (start us, length us, event | category | flops | bytes accessed | tf_op | source)
XLA Modules:
  0.0 695.1 jit_solution(9276019483652715411)
XLA Ops:
  7.2 2.1 collective-permute-start.1
  9.3 3.6 collective-permute-done.1
  12.9 3.9 collective-permute-start.2
  16.9 3.1 collective-permute-done.2
  19.9 7.5 %collective-permute-start.3 = (bf16[2,128,384]{2,1,0:T(8,128)(2,1)S(1)}, bf16[2,128,384]{2,1,0:T(8,128)(2,1)S(1)}, u32[]{:S(2)}, u32[]{:S(2)}) collective-permute-start(bf16[2,128,384]{2,1,0:T(8,128)(2,1)S(1)} %collective-permute-done.2), channel_id=1, source_target_pairs={{0,128},{32,160},{64,192},{96,224},{128,0},{160,32},{192,64},{224,... | collective-permute-start | bytes 589832 | tf_op jit(solution)/shard_map/ppermute | solution.py:13
  27.4 3.2 collective-permute-done.3
  30.5 0.7 fusion.85
  31.3 0.7 all-gather.10.cloned.1.call-update
  32.0 0.7 all-gather.14.cloned.1.call-update
  32.8 68.2 %all-gather.12.cloned.1.call-done = bf16[1,128,12288]{2,1,0:T(8,128)(2,1)} async-done(((bf16[1,128,384]{2,1,0:T(8,128)(2,1)}), bf16[1,128,12288]{2,1,0:T(8,128)(2,1)}) %all-gather.12.cloned.1.call-update) | async-done | bytes 3145744 | tf_op jit(solution)/shard_map/all_gather | solution.py:73
  101.0 2.7 fusion.18
  103.8 6.8 fusion.40
  110.6 3.0 convolution_convert_fusion.1
  113.7 2.9 copy.12
  116.6 47.0 %all-gather.10.cloned.1.call-done = bf16[1,128,12288]{2,1,0:T(8,128)(2,1)} async-done(((bf16[1,128,384]{2,1,0:T(8,128)(2,1)}), bf16[1,128,12288]{2,1,0:T(8,128)(2,1)}) %all-gather.10.cloned.1.call-update) | async-done | bytes 3145744 | tf_op jit(solution)/shard_map/all_gather | solution.py:73
  163.7 2.6 fusion.15
  166.3 6.6 fusion.52
  172.9 3.1 collective-permute-start
  176.0 1.9 collective-permute-done
  177.9 0.7 broadcast_select_fusion.1
  178.7 48.0 %all-gather.14.cloned.1.call-done = bf16[1,128,12288]{2,1,0:T(8,128)(2,1)} async-done(((bf16[1,128,384]{2,1,0:T(8,128)(2,1)}), bf16[1,128,12288]{2,1,0:T(8,128)(2,1)}) %all-gather.14.cloned.1.call-update) | async-done | bytes 3145744 | tf_op jit(solution)/shard_map/all_gather | solution.py:73
  226.7 2.7 fusion.21
  229.4 141.3 %reduce-scatter.7.cloned.1.call-done = bf16[384,128]{1,0:T(8,128)(2,1)} async-done(((bf16[12288,128]{1,0:T(8,128)(2,1)}), bf16[384,128]{1,0:T(8,128)(2,1)}) %reduce-scatter.7.cloned.1.call-update) | async-done | bytes 98320
  370.7 1.0 copy.13
  371.8 73.2 %psum.14 = f32[128]{0:T(128)S(1)} all-reduce(f32[128]{0:T(128)S(1)} %fusion.43), channel_id=1, replica_groups=mesh['section'=8,'tp'=32] {'tp'}, use_global_device_ids=true, to_apply=%region_5.6 | all-reduce | flops 128 | bytes 1024 | tf_op jit(solution)/shard_map/psum | solution.py:56
  444.9 0.1 fusion.42
  445.1 1.5 collective-permute-start.4
  446.6 4.0 collective-permute-done.4
  450.6 6.8 fusion.37
  457.4 0.3 slice-done.5
  457.7 4.7 convolution_convert_fusion
  462.5 4.7 copy.14
  467.2 1.5 collective-permute-start.5
  468.8 1.9 collective-permute-done.5
  470.7 11.0 %collective-permute-start.6 = (bf16[128,384]{1,0:T(8,128)(2,1)S(1)}, bf16[128,384]{1,0:T(8,128)(2,1)S(1)}, u32[]{:S(2)}, u32[]{:S(2)}) collective-permute-start(bf16[128,384]{1,0:T(8,128)(2,1)S(1)} %collective-permute-done.5), channel_id=1, source_target_pairs={{0,64},{32,96},{64,0},{96,32},{128,192},{160,224},{192,128},{224,1... | collective-permute-start | bytes 294920 | tf_op jit(solution)/shard_map/ppermute | solution.py:13
  481.7 2.5 collective-permute-start.9
  484.2 1.3 collective-permute-done.6
  485.5 2.6 collective-permute-done.9
  488.1 2.8 collective-permute-start.10
  490.9 2.5 collective-permute-done.7
  493.4 2.1 collective-permute-done.10
  495.5 0.7 maximum_bitcast_fusion
  496.2 2.6 fusion.12
  498.8 7.3 %fusion.81 = bf16[1,128,384]{2,1,0:T(8,128)(2,1)} fusion(bf16[128,384]{1,0:T(8,128)(2,1)S(1)} %copy-done, bf16[1,12288,384]{2,1,0:T(8,128)(2,1)} %param.12, bf16[128,12288]{1,0:T(8,128)(2,1)} %all-gather.8.cloned.1.call-done, f32[128]{0:T(128)S(1)} %add_sqrt_fusion.2, f32[12288]{0:T(1024)S(1)} %bitcast.97), kind=kOutput, calls=%fused_computation.92 | convolution fusion | flops 1214791680 | bytes 12829184 | tf_op jit(solution)/shard_map/dot_general | solution.py:37
  506.0 107.7 %reduce-scatter.9.cloned.1.call-done = bf16[384,128]{1,0:T(8,128)(2,1)} async-done(((bf16[12288,128]{1,0:T(8,128)(2,1)}), bf16[384,128]{1,0:T(8,128)(2,1)}) %reduce-scatter.9.cloned.1.call-update) | async-done | bytes 98320
  613.7 1.0 copy.15
  614.8 72.6 %psum.15 = f32[128]{0:T(128)S(1)} all-reduce(f32[128]{0:T(128)S(1)} %fusion.45), channel_id=1, replica_groups=mesh['section'=8,'tp'=32] {'tp'}, use_global_device_ids=true, to_apply=%region_9.10 | all-reduce | flops 128 | bytes 1024 | tf_op jit(solution)/shard_map/psum | solution.py:56
  687.5 0.8 fusion.82
  (50 shorter events, 0.8 us)
Async XLA Ops:
  7.2 93.8 %all-gather.12.cloned.1.call-start = ((), (), s32[]{:S(2)}) async-start(), calls=%async_computation.4 | async-start | bytes 3244032 | tf_op jit(solution)/shard_map/all_gather | solution.py:73
  7.2 5.7 collective-permute-start.1
  12.9 7.0 %collective-permute-start.2 = (bf16[2,128,384]{2,1,0:T(8,128)(2,1)S(1)}, bf16[2,128,384]{2,1,0:T(8,128)(2,1)S(1)}, u32[]{:S(2)}, u32[]{:S(2)}) collective-permute-start(bf16[2,128,384]{2,1,0:T(8,128)(2,1)S(1)} %collective-permute-done.1), channel_id=1, source_target_pairs={{0,64},{32,96},{64,0},{96,32},{128,192},{160,224},{192,128},{224,1... | collective-permute-start | bytes 589832 | tf_op jit(solution)/shard_map/ppermute | solution.py:13
  19.9 10.6 %collective-permute-start.3 = (bf16[2,128,384]{2,1,0:T(8,128)(2,1)S(1)}, bf16[2,128,384]{2,1,0:T(8,128)(2,1)S(1)}, u32[]{:S(2)}, u32[]{:S(2)}) collective-permute-start(bf16[2,128,384]{2,1,0:T(8,128)(2,1)S(1)} %collective-permute-done.2), channel_id=1, source_target_pairs={{0,128},{32,160},{64,192},{96,224},{128,0},{160,32},{192,64},{224,... | collective-permute-start | bytes 589832 | tf_op jit(solution)/shard_map/ppermute | solution.py:13
  31.2 132.4 %all-gather.10.cloned.1.call-start = ((), (), s32[]{:S(2)}) async-start(), calls=%async_computation.3 | async-start | bytes 3244032 | tf_op jit(solution)/shard_map/all_gather | solution.py:73
  32.0 194.7 %all-gather.14.cloned.1.call-start = ((), (), s32[]{:S(2)}) async-start(), calls=%async_computation.5 | async-start | bytes 3244032 | tf_op jit(solution)/shard_map/all_gather | solution.py:73
  32.7 337.9 %reduce-scatter.7.cloned.1.call-start = ((), (), s32[]{:S(2)}) async-start(), calls=%async_computation.6 | async-start | bytes 3244032
  101.0 9.6 %slice-start = ((s8[9437184]{0:T(1024)(128)(4,1)}), s8[4194304]{0:T(1024)(128)(4,1)S(1)}, s32[]{:S(2)}) async-start(s8[9437184]{0:T(1024)(128)(4,1)} %bitcast.82), calls=%async_computation.8 | async-start | bytes 8388608
  103.7 6.8 slice-start.1
  103.8 6.8 slice-start.2
  113.6 52.6 %copy-start.1 = (bf16[1,128,384]{2,1,0:T(8,128)(2,1)S(1)}, bf16[1,128,384]{2,1,0:T(8,128)(2,1)}, u32[]{:S(2)}) copy-start(bf16[1,128,384]{2,1,0:T(8,128)(2,1)} %param.8) | copy-start | bytes 294916
  113.6 52.6 %copy-start.6 = (f32[1,12288]{1,0:T(1,128)S(1)}, f32[1,12288]{1,0:T(1,128)}, u32[]{:S(2)}) copy-start(f32[1,12288]{1,0:T(1,128)} %param.13) | copy-start | bytes 147460
  116.6 379.6 %all-gather.8.cloned.1.call-start = ((), (), s32[]{:S(2)}) async-start(), calls=%async_computation.2 | async-start | bytes 3244032 | tf_op jit(solution)/shard_map/all_gather | solution.py:73
  166.3 11.7 %copy-start.2 = (bf16[128,384]{1,0:T(8,128)(2,1)S(1)}, bf16[128,384]{1,0:T(8,128)(2,1)}, u32[]{:S(2)}) copy-start(bf16[128,384]{1,0:T(8,128)(2,1)} %param.7) | copy-start | bytes 294916
  166.3 278.7 %copy-start.3 = (bf16[1,128,384]{2,1,0:T(8,128)(2,1)S(1)}, bf16[1,128,384]{2,1,0:T(8,128)(2,1)}, u32[]{:S(2)}) copy-start(bf16[1,128,384]{2,1,0:T(8,128)(2,1)} %param.10) | copy-start | bytes 294916
  166.3 284.3 %copy-start.5 = (bf16[128,384]{1,0:T(8,128)(2,1)S(1)}, bf16[128,384]{1,0:T(8,128)(2,1)}, u32[]{:S(2)}) copy-start(bf16[128,384]{1,0:T(8,128)(2,1)} %param.9) | copy-start | bytes 294916
  172.9 284.5 %copy-start.7 = (bf16[128,384]{1,0:T(8,128)(2,1)}, bf16[128,384]{1,0:T(8,128)(2,1)S(1)}, u32[]{:S(2)}) copy-start(bf16[128,384]{1,0:T(8,128)(2,1)S(1)} %fusion.52) | copy-start | bytes 294916
  172.9 5.0 collective-permute-start
  178.6 435.1 %reduce-scatter.9.cloned.1.call-start = ((), (), s32[]{:S(2)}) async-start(), calls=%async_computation.7 | async-start | bytes 3244032
  226.7 230.7 %slice-start.3 = ((s8[9437184]{0:T(1024)(128)(4,1)}), s8[1048576]{0:T(1024)(128)(4,1)S(1)}, s32[]{:S(2)}) async-start(s8[9437184]{0:T(1024)(128)(4,1)} %bitcast.84), calls=%async_computation.11 | async-start | bytes 2097152
  445.1 12.3 %copy-start.4 = (bf16[128,384]{1,0:T(8,128)(2,1)}, bf16[128,384]{1,0:T(8,128)(2,1)S(1)}, u32[]{:S(2)}) copy-start(bf16[128,384]{1,0:T(8,128)(2,1)S(1)} %fusion.42) | copy-start | bytes 294916
  445.1 5.5 collective-permute-start.4
  450.6 6.8 slice-start.4
  450.6 7.1 %slice-start.5 = ((s8[9437184]{0:T(1024)(128)(4,1)}), s8[4194304]{0:T(1024)(128)(4,1)S(1)}, s32[]{:S(2)}) async-start(s8[9437184]{0:T(1024)(128)(4,1)} %bitcast.84), calls=%async_computation.13 | async-start | bytes 8388608
  462.5 6.3 copy-start
  467.2 3.6 collective-permute-start.5
  468.7 13.0 %collective-permute-start.8 = (bf16[128,384]{1,0:T(8,128)(2,1)S(1)}, bf16[128,384]{1,0:T(8,128)(2,1)S(1)}, u32[]{:S(2)}, u32[]{:S(2)}) collective-permute-start(bf16[128,384]{1,0:T(8,128)(2,1)S(1)} %copy-done), channel_id=1, source_target_pairs={{0,32},{32,0},{64,96},{96,64},{128,160},{160,128},{192,224},{224,1... | collective-permute-start | bytes 294920 | tf_op jit(solution)/shard_map/ppermute | solution.py:13
  470.7 14.7 %collective-permute-start.6 = (bf16[128,384]{1,0:T(8,128)(2,1)S(1)}, bf16[128,384]{1,0:T(8,128)(2,1)S(1)}, u32[]{:S(2)}, u32[]{:S(2)}) collective-permute-start(bf16[128,384]{1,0:T(8,128)(2,1)S(1)} %collective-permute-done.5), channel_id=1, source_target_pairs={{0,64},{32,96},{64,0},{96,32},{128,192},{160,224},{192,128},{224,1... | collective-permute-start | bytes 294920 | tf_op jit(solution)/shard_map/ppermute | solution.py:13
  481.7 6.4 collective-permute-start.9
  485.5 7.9 %collective-permute-start.7 = (bf16[128,384]{1,0:T(8,128)(2,1)S(1)}, bf16[128,384]{1,0:T(8,128)(2,1)S(1)}, u32[]{:S(2)}, u32[]{:S(2)}) collective-permute-start(bf16[128,384]{1,0:T(8,128)(2,1)S(1)} %collective-permute-done.6), channel_id=1, source_target_pairs={{0,128},{32,160},{64,192},{96,224},{128,0},{160,32},{192,64},{224,... | collective-permute-start | bytes 294920 | tf_op jit(solution)/shard_map/ppermute | solution.py:13
  488.1 7.4 %collective-permute-start.10 = (bf16[128,384]{1,0:T(8,128)(2,1)S(1)}, bf16[128,384]{1,0:T(8,128)(2,1)S(1)}, u32[]{:S(2)}, u32[]{:S(2)}) collective-permute-start(bf16[128,384]{1,0:T(8,128)(2,1)S(1)} %collective-permute-done.9), channel_id=1, source_target_pairs={{0,128},{32,160},{64,192},{96,224},{128,0},{160,32},{192,64},{224,... | collective-permute-start | bytes 294920 | tf_op jit(solution)/shard_map/ppermute | solution.py:13
Sparse Core Ops, SparseCore 0:
  31.4 69.5 all-gather.11
  102.8 60.8 all-gather.9
  166.1 60.5 all-gather.13
  229.1 141.5 reduce-scatter.6
  373.0 64.8 all-gather.7
  467.3 146.3 reduce-scatter.8
where the time goes:
time: 695 us
  waiting for transfers between devices  440 us (63%)
  blocking collectives  146 us (21%)
  starting transfers between devices  36.2 us (5%)
  matrix products  35.2 us (5%)
  between operations  14.4 us (2%)
  other arithmetic  13.1 us (2%)
  local copies, waits for them, and re-layouts  10.7 us (2%)
    unnamed x8, waiting for transfers between devices  250 us
    all_gather x4, waiting for transfers between devices, gather_rows(): return lax.all_gather(part_rows, 'tp', axis=1, tiled=True)  163 us
    psum x2, blocking collectives, backward(): lax.psum(jnp.sum(dnorm * g_local[None, :] * own_f, axis=-1, keepdims=True...  146 us
    ppermute x9, starting transfers between devices, from_partner(): return lax.ppermute(value, axis, pairs)  31.4 us
    dot_general x4, matrix products, layer_parts(): hidden = jnp.dot(normed, w_cols, preferred_element_type=jnp.float32)  27.4 us
    ppermute x9, waiting for transfers between devices, from_partner(): return lax.ppermute(value, axis, pairs)  20.2 us
  transfers between devices with their start and end apart: 17, of which 15 were waited for; matrix products, arithmetic and copies ran while one was open for 8% of the time, Pallas kernels for 0%

commit v1 on v0

v1 whole, which is shorter than its diff:
```python
import functools

import jax
import jax.numpy as jnp
from jax import lax
from jax.experimental import pallas as pl
from jax.experimental.pallas import tpu as pltpu
from jax.sharding import PartitionSpec as P

EPS = 1e-05
GCOEF = 0.7978845608028654
MESH = pl.DeviceIdType.MESH

TOK = 128
W = 384
NZ = 4
NY = 4
HALF = TOK // 2
A, B, C, D = 0, 1, 2, 3
BF = jnp.bfloat16
F32 = jnp.float32


def gelu_value(h):
    return 0.5 * h * (1.0 + jnp.tanh(GCOEF * (h + 0.044715 * h * h * h)))


def gelu_slope(h):
    tval = jnp.tanh(GCOEF * (h + 0.044715 * h * h * h))
    return 0.5 * (1.0 + tval) + 0.5 * h * (1.0 - tval * tval) * GCOEF * (
        1.0 + 3.0 * 0.044715 * h * h
    )


def kernel(
    nsec,
    fresh_in, fwd_in, fresh_cot, cot_in, stash_in, weight, gain,
    first_out, second_out, first_grad, second_grad, stash_out,
    xg, wc, gv, acc, hr, uu, cot, outb, rb,
    hsend, hin, fsend, fin, zsend, zin, dnacc, qown, qc, qy, qz, qsum,
    s_z, r_z, s_y, r_y, s_r, r_r,
    s_w, r_w, l_w,
    s_h, r_h, s_u, r_u,
    s_ev, r_ev, s_next, r_next, s_prev, r_prev, s_st, r_st,
    l_in, l_out,
    s_a, r_a, s_b, r_b, s_c, r_c,
    s_q, r_q,
):
    sec = lax.axis_index("section")
    tp = lax.axis_index("tp")
    core = lax.rem(tp, 2)
    y = lax.rem(tp // 2, NY)
    z = tp // (2 * NY)
    width = NZ * NY * 2 * W

    def at(zz, yy, cc=None):
        return (sec, (zz * NY + yy) * 2 + (core if cc is None else cc))

    def turn(v, k, n):
        return lax.rem(v + k, n)

    yr, yl, yo = turn(y, 1, NY), turn(y, 3, NY), turn(y, 2, NY)
    right, left, over = at(z, yr), at(z, yl), at(z, yo)
    twin = at(z, y, 1 - core)
    mirror = (nsec - 1 - sec, tp)
    after = (turn(sec, 1, nsec), tp)
    before = (turn(sec, nsec - 1, nsec), tp)

    def far(src, dst, ssem, rsem, dev):
        return pltpu.make_async_remote_copy(
            src_ref=src, dst_ref=dst, send_sem=ssem, recv_sem=rsem,
            device_id=dev, device_id_type=MESH,
        )

    def arrived(dst, ssem, rsem):
        far(dst, dst, ssem, rsem, twin).wait_recv()

    def sent(src, ssem, rsem):
        far(src, src, ssem, rsem, twin).wait_send()

    def near(src, dst, sem):
        return pltpu.make_async_copy(src, dst, sem)

    barrier = pltpu.get_barrier_semaphore()

    def greet(dev):
        pl.semaphore_signal(barrier, inc=1, device_id=dev, device_id_type=MESH)

    for k in range(1, NZ):
        greet(at(turn(z, k, NZ), y))
    for dev in (right, left, over, twin, mirror, after, before):
        greet(dev)
    pl.semaphore_wait(barrier, 10)

    def own_sends(g, src):
        for k in range(1, NZ):
            far(src, xg.at[g, y, z], s_z.at[g, k], r_z.at[g, z],
                at(turn(z, k, NZ), y)).start()
        far(src, xg.at[g, y, z], s_y.at[g, z, 0], r_y.at[g, z, 0], right).start()
        far(src, xg.at[g, y, z], s_y.at[g, z, 1], r_y.at[g, z, 1], left).start()

    def column_sends(g):
        def body(i, carry):
            zq = turn(z, i, NZ)
            slot = xg.at[g, y, zq]
            arrived(slot, s_z.at[g, 0], r_z.at[g, zq])
            far(slot, slot, s_y.at[g, zq, 0], r_y.at[g, zq, 0], right).start()
            far(slot, slot, s_y.at[g, zq, 1], r_y.at[g, zq, 1], left).start()
            return carry
        lax.fori_loop(1, NZ, body, 0)

    def product(g, yy, zq):
        x = xg[g, yy, zq].astype(F32)
        x2 = x * x
        acc[g, :, 2 * W:] += x2[:, :128] + x2[:, 128:256] + x2[:, 256:]
        start = pl.multiple_of(((zq * NY + yy) * 2 + core) * W, 128)
        n = (x * gv[:, pl.ds(start, W)]).astype(BF)
        acc[g, :, :2 * W] += jnp.dot(n, wc[yy, zq], preferred_element_type=F32)

    def relay(g):
        def body(i, carry):
            zq = turn(z, i, NZ)
            from_left, from_right = xg.at[g, yl, zq], xg.at[g, yr, zq]
            product(g, y, zq)
            arrived(from_left, s_z.at[g, 0], r_y.at[g, zq, 0])
            top = from_left.at[pl.ds(0, HALF)]
            far(top, top, s_r.at[g, zq, 0], r_r.at[g, zq, 0], right).start()
            arrived(from_right, s_z.at[g, 0], r_y.at[g, zq, 1])
            low = from_right.at[pl.ds(HALF, HALF)]
            far(low, low, s_r.at[g, zq, 1], r_r.at[g, zq, 1], left).start()
            product(g, yl, zq)
            product(g, yr, zq)
            return carry
        lax.fori_loop(0, NZ, body, 0)

    def last_quarter(g):
        def body(i, carry):
            zq = turn(z, i, NZ)
            slot = xg.at[g, yo, zq]
            arrived(slot.at[pl.ds(0, HALF)], s_z.at[g, 0], r_r.at[g, zq, 0])
            arrived(slot.at[pl.ds(HALF, HALF)], s_z.at[g, 0], r_r.at[g, zq, 1])
            product(g, yo, zq)
            return carry
        lax.fori_loop(0, NZ, body, 0)
        far(acc.at[g, :, pl.ds(W, W + 128)], hr.at[g], s_h.at[g], r_h.at[g], twin).start()

    def hidden(g):
        arrived(hr.at[g], s_z.at[g, 0], r_h.at[g])
        ss = acc[g, :, 2 * W:] + hr[g, :, W:]
        radius = jnp.sqrt(jnp.sum(ss, axis=-1, keepdims=True) / width + EPS)
        h = (acc[g, :, :W] + hr[g, :, :W]) / radius
        return radius, h

    def part(b, yy, zq):
        return lax.dot_general(
            uu[b], wc[yy, zq], (((1,), (1,)), ((), ())), preferred_element_type=F32
        )

    def gradient_start(b, g):
        radius, h = hidden(g)
        u = (cot[b].astype(F32) * gelu_slope(h)).astype(BF)
        uu[b, :, :W] = u
        far(uu.at[b, :, pl.ds(0, W)], uu.at[b, :, pl.ds(W, W)], s_u.at[b], r_u.at[b], twin).start()
        rb[b] = jnp.broadcast_to(radius, (TOK, 128))
        e = u.astype(F32) * h
        lanes = (e[:, :128] + e[:, 128:256] + e[:, 256:]) * radius
        t = lanes.T
        q = t[0:8]
        for k in range(1, 16):
            q = q + t[8 * k:8 * k + 8]
        qown[b] = q
        far(qown.at[b], qc.at[b], s_q.at[b, 0], r_q.at[b, 0], twin).start()
        arrived(uu.at[b, :, pl.ds(W, W)], s_u.at[b], r_u.at[b])

    def scatter_over(b):
        def body(i, carry):
            zq = turn(z, i, NZ)
            hsend[b, zq] = part(b, yo, zq).astype(BF)
            far(hsend.at[b, zq, pl.ds(0, HALF)], hin.at[b, zq, pl.ds(0, HALF)],
                s_a.at[b, zq, 0], r_a.at[b, zq, 0], right).start()
            far(hsend.at[b, zq, pl.ds(HALF, HALF)], hin.at[b, zq, pl.ds(HALF, HALF)],
                s_a.at[b, zq, 1], r_a.at[b, zq, 1], left).start()
            return carry
        lax.fori_loop(1, NZ + 1, body, 0)

    def scatter_sides(b):
        arrived(qc.at[b], s_q.at[b, 0], r_q.at[b, 0])
        qsum[b, 0] = qown[b] + qc[b]
        for k in range(1, NY):
            far(qsum.at[b, 0], qy.at[b, k], s_q.at[b, k], r_q.at[b, k],
                at(z, turn(y, k, NY))).start()

        def body(i, carry):
            zq = turn(z, i, NZ)
            to_right = part(b, yr, zq)
            arrived(hin.at[b, zq, pl.ds(0, HALF)], s_a.at[b, zq, 0], r_a.at[b, zq, 0])
            fsend[b, zq, 0, :HALF] = (to_right[:HALF] + hin[b, zq, :HALF].astype(F32)).astype(BF)
            fsend[b, zq, 0, HALF:] = to_right[HALF:].astype(BF)
            far(fsend.at[b, zq, 0], fin.at[b, zq, 0], s_b.at[b, zq, 0], r_b.at[b, zq, 0], right).start()
            to_left = part(b, yl, zq)
            arrived(hin.at[b, zq, pl.ds(HALF, HALF)], s_a.at[b, zq, 1], r_a.at[b, zq, 1])
            fsend[b, zq, 1, :HALF] = to_left[:HALF].astype(BF)
            fsend[b, zq, 1, HALF:] = (to_left[HALF:] + hin[b, zq, HALF:].astype(F32)).astype(BF)
            far(fsend.at[b, zq, 1], fin.at[b, zq, 1], s_b.at[b, zq, 1], r_b.at[b, zq, 1], left).start()
            return carry
        lax.fori_loop(1, NZ + 1, body, 0)

    def own_column(b, zq):
        mine = part(b, y, zq)
        arrived(fin.at[b, zq, 0], s_b.at[b, zq, 0], r_b.at[b, zq, 0])
        arrived(fin.at[b, zq, 1], s_b.at[b, zq, 1], r_b.at[b, zq, 1])
        return mine + fin[b, zq, 0].astype(F32) + fin[b, zq, 1].astype(F32)

    def scatter_column(b):
        total = qsum[b, 0]
        for k in range(1, NY):
            arrived(qy.at[b, k], s_q.at[b, k], r_q.at[b, k])
            total = total + qy[b, k]
        qsum[b, 1] = total
        for k in range(1, NZ):
            far(qsum.at[b, 1], qz.at[b, k], s_q.at[b, 3 + k], r_q.at[b, 3 + k],
                at(turn(z, k, NZ), y)).start()

        def body(i, carry):
            zq = turn(z, i, NZ)
            zsend[b, zq] = own_column(b, zq).astype(BF)
            far(zsend.at[b, zq], zin.at[b, z], s_c.at[b, zq], r_c.at[b, z], at(zq, y)).start()
            return carry
        lax.fori_loop(1, NZ, body, 0)
        dnacc[...] = own_column(b, z)

    def gradient_end(b, g):
        total = qsum[b, 1]
        for k in range(1, NZ):
            arrived(qz.at[b, k], s_q.at[b, 3 + k], r_q.at[b, 3 + k])
            total = total + qz[b, k]
        row = jnp.sum(total, axis=0, keepdims=True)
        inner = jnp.broadcast_to(row, (128, TOK)).T[:, :1]
        dn = dnacc[...]
        for k in range(1, NZ):
            zq = turn(z, k, NZ)
            arrived(zin.at[b, zq], s_c.at[b, zq], r_c.at[b, zq])
            dn = dn + zin[b, zq].astype(F32)
        radius = rb[b][:, :1]
        mine = pl.multiple_of(tp * W, 128)
        x = xg[g, y, z].astype(F32)
        grad = (
            cot[b].astype(F32)
            + gv[:, pl.ds(mine, W)] * dn / radius
            - x * (inner / (width * radius * radius * radius))
        )
        outb[2 + b] = grad.astype(BF)

    def forward_end(g, slot):
        radius, h = hidden(g)
        outb[slot] = (xg[g, y, z].astype(F32) + gelu_value(h)).astype(BF)

    own_sends(B, fwd_in.at[0])
    far(stash_in.at[0, 0], xg.at[A, y, z], s_ev.at[0], r_ev.at[0], mirror).start()
    near(fwd_in.at[0], xg.at[B, y, z], l_in.at[0]).start()
    near(gain, gv, l_in.at[1]).start()
    near(cot_in.at[0], cot.at[0], l_in.at[2]).start()
    for k, yy in enumerate((y, yl, yr, yo)):
        near(weight.at[:, yy, core], wc.at[yy, :, :, pl.ds(0, W)], l_w.at[k]).start()
        far(weight.at[:, yy, 1 - core], wc.at[yy, :, :, pl.ds(W, W)], s_w.at[k], r_w.at[k], twin).start()
    far(stash_in.at[0, 1], xg.at[C, y, z], s_ev.at[1], r_ev.at[1], mirror).start()
    far(fwd_in.at[0], stash_out.at[0, 0], s_st.at[0], r_st.at[0], mirror).start()

    @pl.when(sec == 0)
    def _():
        near(fresh_in, xg.at[D, y, z], l_in.at[3]).start()

    @pl.when(sec == nsec - 1)
    def _():
        near(fresh_cot, cot.at[1], l_in.at[4]).start()

    acc[...] = jnp.zeros_like(acc)
    column_sends(B)
    near(fwd_in.at[0], xg.at[B, y, z], l_in.at[0]).wait()
    near(gain, gv, l_in.at[1]).wait()
    near(cot_in.at[0], cot.at[0], l_in.at[2]).wait()
    arrived(xg.at[A, y, z], s_ev.at[0], r_ev.at[0])
    own_sends(A, xg.at[A, y, z])
    for k, yy in enumerate((y, yl, yr, yo)):
        near(weight.at[:, yy, core], wc.at[yy, :, :, pl.ds(0, W)], l_w.at[k]).wait()
        arrived(wc.at[yy, :, :, pl.ds(W, W)], s_w.at[k], r_w.at[k])
    relay(B)
    column_sends(A)
    last_quarter(B)
    arrived(xg.at[C, y, z], s_ev.at[1], r_ev.at[1])
    own_sends(C, xg.at[C, y, z])
    forward_end(B, 0)

    @pl.when(sec < nsec - 1)
    def _():
        far(outb.at[0], xg.at[D, y, z], s_next, r_next, after).start()

    near(outb.at[0], first_out.at[0], l_out.at[0]).start()
    relay(A)
    column_sends(C)
    last_quarter(A)

    @pl.when(sec == 0)
    def _():
        near(fresh_in, xg.at[D, y, z], l_in.at[3]).wait()

    @pl.when(sec > 0)
    def _():
        arrived(xg.at[D, y, z], s_next, r_next)

    gradient_start(0, A)
    relay(C)
    scatter_over(0)
    last_quarter(C)
    scatter_sides(0)
    own_sends(D, xg.at[D, y, z])
    far(xg.at[D, y, z], stash_out.at[0, 1], s_st.at[1], r_st.at[1], mirror).start()
    column_sends(D)
    scatter_column(0)
    gradient_end(0, A)

    @pl.when(sec > 0)
    def _():
        far(outb.at[2], cot.at[1], s_prev, r_prev, before).start()

    near(outb.at[2], first_grad.at[0], l_out.at[2]).start()
    relay(D)

    @pl.when(sec == nsec - 1)
    def _():
        near(fresh_cot, cot.at[1], l_in.at[4]).wait()

    @pl.when(sec < nsec - 1)
    def _():
        arrived(cot.at[1], s_prev, r_prev)

    gradient_start(1, C)
    scatter_over(1)
    last_quarter(D)
    scatter_sides(1)
    forward_end(D, 1)
    near(outb.at[1], second_out.at[0], l_out.at[1]).start()
    scatter_column(1)
    gradient_end(1, C)
    near(outb.at[3], second_grad.at[0], l_out.at[3]).start()

    for g in range(4):
        own = fwd_in.at[0] if g == B else xg.at[g, y, z]
        for k in range(1, NZ):
            sent(own, s_z.at[g, k], r_z.at[g, z])

        def sends_of(i, carry):
            slot = xg.at[g, 0, i]
            half = slot.at[pl.ds(0, HALF)]
            for k in range(2):
                sent(slot, s_y.at[g, i, k], r_y.at[g, i, k])
                sent(half, s_r.at[g, i, k], r_r.at[g, i, k])
            return carry
        lax.fori_loop(0, NZ, sends_of, 0)
        sent(acc.at[g, :, pl.ds(W, W + 128)], s_h.at[g], r_h.at[g])
    for b in range(2):
        def sends_to(i, carry):
            for k in range(2):
                sent(hsend.at[b, i, pl.ds(0, HALF)], s_a.at[b, i, k], r_a.at[b, i, k])
                sent(fsend.at[b, i, k], s_b.at[b, i, k], r_b.at[b, i, k])
            return carry
        lax.fori_loop(0, NZ, sends_to, 0)

        def sends_up(i, carry):
            zq = turn(z, i, NZ)
            sent(zsend.at[b, zq], s_c.at[b, zq], r_c.at[b, zq])
            return carry
        lax.fori_loop(1, NZ, sends_up, 0)
        sent(uu.at[b, :, pl.ds(0, W)], s_u.at[b], r_u.at[b])
        for k in range(7):
            sent(qown.at[b], s_q.at[b, k], r_q.at[b, k])
        sent(stash_in.at[0, b], s_ev.at[b], r_ev.at[b])
        sent(fwd_in.at[0], s_st.at[b], r_st.at[b])
        arrived(stash_out.at[0, b], s_st.at[b], r_st.at[b])
    for k in range(4):
        sent(weight.at[:, 0, 0], s_w.at[k], r_w.at[k])
    @pl.when(sec < nsec - 1)
    def _():
        sent(outb.at[0], s_next, r_next)

    @pl.when(sec > 0)
    def _():
        sent(outb.at[2], s_prev, r_prev)

    for k, out in enumerate((first_out, second_out, first_grad, second_grad)):
        near(outb.at[k], out.at[0], l_out.at[k]).wait()


def shards(nsec, fresh_in, fwd_in, fresh_cot, cot_in, stash_in, weight, gain):
    weight = weight.reshape(NZ, NY, 2, W, W)
    block = jax.ShapeDtypeStruct((1, TOK, W), BF)
    dma = pltpu.SemaphoreType.DMA
    vm = pltpu.VMEM
    scratch = [
        vm((4, NY, NZ, TOK, W), BF),
        vm((NY, NZ, W, 2 * W), BF),
        vm((1, NY * NZ * 2 * W), F32),
        vm((4, TOK, 2 * W + 128), F32),
        vm((4, TOK, W + 128), F32),
        vm((2, TOK, 2 * W), BF),
        vm((2, TOK, W), BF),
        vm((4, TOK, W), BF),
        vm((2, TOK, 128), F32),
        vm((2, NZ, TOK, W), BF),
        vm((2, NZ, TOK, W), BF),
        vm((2, NZ, 2, TOK, W), BF),
        vm((2, NZ, 2, TOK, W), BF),
        vm((2, NZ, TOK, W), BF),
        vm((2, NZ, TOK, W), BF),
        vm((TOK, W), F32),
        vm((2, 8, 128), F32),
        vm((2, 8, 128), F32),
        vm((2, NY, 8, 128), F32),
        vm((2, NZ, 8, 128), F32),
        vm((2, 2, 8, 128), F32),
        dma((4, NZ)), dma((4, NZ)),
        dma((4, NZ, 2)), dma((4, NZ, 2)),
        dma((4, NZ, 2)), dma((4, NZ, 2)),
        dma((4,)), dma((4,)), dma((4,)),
        dma((4,)), dma((4,)), dma((2,)), dma((2,)),
        dma((2,)), dma((2,)), dma, dma, dma, dma, dma((2,)), dma((2,)),
        dma((5,)), dma((4,)),
        dma((2, NZ, 2)), dma((2, NZ, 2)), dma((2, NZ, 2)), dma((2, NZ, 2)),
        dma((2, NZ)), dma((2, NZ)),
        dma((2, 7)), dma((2, 7)),
    ]
    anywhere = pl.BlockSpec(memory_space=pl.ANY)
    return pl.pallas_call(
        functools.partial(kernel, nsec),
        out_shape=(block, block, block, block, jax.ShapeDtypeStruct((1, 2, TOK, W), BF)),
        in_specs=[anywhere] * 7,
        out_specs=(anywhere,) * 5,
        scratch_shapes=scratch,
        compiler_params=pltpu.CompilerParams(
            collective_id=0, has_side_effects=True, vmem_limit_bytes=56 * 2**20
        ),
        cost_estimate=pl.CostEstimate(flops=7_250_000_000, bytes_accessed=12_000_000, transcendentals=200_000),
    )(fresh_in, fwd_in, fresh_cot, cot_in, stash_in, weight, gain)


def solution(mesh):
    return jax.shard_map(
        functools.partial(shards, mesh.shape["section"]),
        mesh=mesh,
        in_specs=(
            P(None, "tp"),
            P("section", None, "tp"),
            P(None, "tp"),
            P("section", None, "tp"),
            P("section", None, None, "tp"),
            P("section", None, "tp"),
            P("section", None),
        ),
        out_specs=(
            P("section", None, "tp"),
            P("section", None, "tp"),
            P("section", None, "tp"),
            P("section", None, "tp"),
            P("section", None, None, "tp"),
        ),
        check_vma=False,
    )
```

time: 695 us -> 136 us (0.20)
  waiting for transfers between devices: 440 us -> 0 us
  blocking collectives: 146 us -> 0 us
  Pallas kernels: 0 us -> 127 us
  starting transfers between devices: 36.2 us -> 0 us
  matrix products: 35.2 us -> 0 us
  between operations: 14.4 us -> 0.64 us
  other arithmetic: 13.1 us -> 0 us
    unnamed x8 -> x0, waiting for transfers between devices: 250 us -> none
    all_gather x4 -> x0, waiting for transfers between devices: 163 us -> none  [gather_rows(): return lax.all_gather(part_rows, 'tp', axis=1, tiled=True)]
    psum x2 -> x0, blocking collectives: 146 us -> none  [backward(): lax.psum(jnp.sum(dnorm * g_local[None, :] * own_f, axis=-1, keepdims=True...]
    pallas_call x0 -> x1, Pallas kernels: none -> 127 us  [shards(): pl.pallas_call(functools.partial(kernel, nsec), out_shape=(block, block,...]
    ppermute x11 -> x0, starting transfers between devices: 35.9 us -> none  [the longest x9 31.4 us: from_partner(): return lax.ppermute(value, axis, pairs)]
    dot_general x6 -> x0, matrix products: 35.2 us -> none  [the longest x4 27.4 us: layer_parts(): hidden = jnp.dot(normed, w_cols, preferred_element_type=jnp.float32)]
    ppermute x11 -> x0, waiting for transfers between devices: 26.1 us -> none  [the longest x9 20.2 us: from_partner(): return lax.ppermute(value, axis, pairs)]
    reduce_sum x6 -> x0, other arithmetic: 10.8 us -> none  [the longest x4 10.5 us: layer_parts(): radius = jnp.sqrt(jnp.mean(xf * xf, axis=-1, keepdims=True) + EPS)]
  transfers between devices with their start and end apart: 17 -> 0, of which waited for: 15 -> 0; matrix products, arithmetic and copies ran while one was open for 8% -> 0% of each run, Pallas kernels for 0% -> 0%
where the time goes in v1:
time: 136 us
  Pallas kernels  127 us (93%)
  local copies, waits for them, and re-layouts  7.79 us (6%)
    pallas_call x1, Pallas kernels, shards(): pl.pallas_call(functools.partial(kernel, nsec), out_shape=(block, block,...  127 us
    unnamed x5, local copies, waits for them, and re-layouts  7.79 us

profile of v1, /device:TPU:1, one launch (start us, length us, event | category | flops | bytes accessed | tf_op | source)
XLA Modules:
  0.0 135.6 jit_solution(10781932188747280468)
XLA Ops:
  0.6 127.2 %shard_map.110 = (bf16[1,128,384]{2,1,0:T(8,128)(2,1)}, bf16[1,128,384]{2,1,0:T(8,128)(2,1)}, bf16[1,128,384]{2,1,0:T(8,128)(2,1)}, bf16[1,128,384]{2,1,0:T(8,128)(2,1)}, bf16[1,2,128,384]{3,2,1,0:T(8,128)(2,1)}) custom-call(bf16[128,384]{1,0:T(8,128)(2,1)} %fresh_in.1, bf16[1,128,384]{2,1,0:T(8,128)(2,1)} %fwd_in.1, bf16[128,384]{1,0:T(8,128)(2,1)} %fresh_cot.1, ...), custom_call_target="tpu_custom_call" | custom-call | flops 7249999872 | bytes 12000000 | tf_op jit(solution)/shard_map/pallas_call | solution.py:433
  127.8 1.5 %copy.17 = bf16[1,128,384]{2,1,0:T(8,128)(2,1)} copy(bf16[1,128,384]{2,1,0:T(8,128)(2,1)} %get-tuple-element.10) | data formatting | bytes 196608
  129.4 1.5 %copy.18 = bf16[1,128,384]{2,1,0:T(8,128)(2,1)} copy(bf16[1,128,384]{2,1,0:T(8,128)(2,1)} %get-tuple-element.11) | data formatting | bytes 196608
  130.9 1.5 %copy.19 = bf16[1,128,384]{2,1,0:T(8,128)(2,1)} copy(bf16[1,128,384]{2,1,0:T(8,128)(2,1)} %get-tuple-element.12) | data formatting | bytes 196608
  132.4 1.5 %copy.20 = bf16[1,128,384]{2,1,0:T(8,128)(2,1)} copy(bf16[1,128,384]{2,1,0:T(8,128)(2,1)} %get-tuple-element.13) | data formatting | bytes 196608
  134.0 1.6 %copy.21 = bf16[1,2,128,384]{3,2,1,0:T(8,128)(2,1)} copy(bf16[1,2,128,384]{3,2,1,0:T(8,128)(2,1)} %get-tuple-element.14) | data formatting | bytes 393216

commit v2 on v1

--- a/solution.py
+++ b/solution.py
@@ -81,6 +81,8 @@
     def near(src, dst, sem):
         return pltpu.make_async_copy(src, dst, sem)
 
+    for k, yy in enumerate((y, yl, yr, yo)):
+        near(weight.at[:, yy, core], wc.at[yy, :, :, pl.ds(0, W)], l_w.at[k]).start()
     barrier = pltpu.get_barrier_semaphore()
 
     def greet(dev):
@@ -92,18 +94,45 @@
         greet(dev)
     pl.semaphore_wait(barrier, 10)
 
-    def own_sends(g, src):
-        for k in range(1, NZ):
-            far(src, xg.at[g, y, z], s_z.at[g, k], r_z.at[g, z],
-                at(turn(z, k, NZ), y)).start()
+    below, above = at(turn(z, 3, NZ), y), at(turn(z, 1, NZ), y)
+
+    def nearest(i):
+        v = jnp.where((z == 0) | (z == 3), i, jnp.where(i < 2, 1 - i, i))
+        return jnp.where(z < 2, v, 3 - v)
+
+    def go_up(g, src, zq):
+        far(src, xg.at[g, y, zq], s_z.at[g, zq, 0], r_z.at[g, zq], above).start()
+
+    def go_down(g, src, zq):
+        far(src, xg.at[g, y, zq], s_z.at[g, zq, 1], r_z.at[g, zq], below).start()
+
+    def own_up(g, src):
+        @pl.when(z < NZ - 1)
+        def _():
+            go_up(g, src, z)
+
+        @pl.when(z > 0)
+        def _():
+            go_down(g, src, z)
+
+    def own_across(g, src):
         far(src, xg.at[g, y, z], s_y.at[g, z, 0], r_y.at[g, z, 0], right).start()
         far(src, xg.at[g, y, z], s_y.at[g, z, 1], r_y.at[g, z, 1], left).start()
 
     def column_sends(g):
         def body(i, carry):
-            zq = turn(z, i, NZ)
+            zq = nearest(i)
             slot = xg.at[g, y, zq]
-            arrived(slot, s_z.at[g, 0], r_z.at[g, zq])
+            arrived(slot, s_z.at[g, 0, 0], r_z.at[g, zq])
+
+            @pl.when((zq < z) & (z < NZ - 1))
+            def _():
+                go_up(g, slot, zq)
+
+            @pl.when((zq > z) & (z > 0))
+            def _():
+                go_down(g, slot, zq)
+
             far(slot, slot, s_y.at[g, zq, 0], r_y.at[g, zq, 0], right).start()
             far(slot, slot, s_y.at[g, zq, 1], r_y.at[g, zq, 1], left).start()
             return carry
@@ -119,15 +148,15 @@
 
     def relay(g):
         def body(i, carry):
-            zq = turn(z, i, NZ)
+            zq = nearest(i)
             from_left, from_right = xg.at[g, yl, zq], xg.at[g, yr, zq]
-            product(g, y, zq)
-            arrived(from_left, s_z.at[g, 0], r_y.at[g, zq, 0])
+            arrived(from_left, s_z.at[g, 0, 0], r_y.at[g, zq, 0])
             top = from_left.at[pl.ds(0, HALF)]
             far(top, top, s_r.at[g, zq, 0], r_r.at[g, zq, 0], right).start()
-            arrived(from_right, s_z.at[g, 0], r_y.at[g, zq, 1])
+            arrived(from_right, s_z.at[g, 0, 0], r_y.at[g, zq, 1])
             low = from_right.at[pl.ds(HALF, HALF)]
             far(low, low, s_r.at[g, zq, 1], r_r.at[g, zq, 1], left).start()
+            product(g, y, zq)
             product(g, yl, zq)
             product(g, yr, zq)
             return carry
@@ -135,17 +164,17 @@
 
     def last_quarter(g):
         def body(i, carry):
-            zq = turn(z, i, NZ)
+            zq = nearest(i)
             slot = xg.at[g, yo, zq]
-            arrived(slot.at[pl.ds(0, HALF)], s_z.at[g, 0], r_r.at[g, zq, 0])
-            arrived(slot.at[pl.ds(HALF, HALF)], s_z.at[g, 0], r_r.at[g, zq, 1])
+            arrived(slot.at[pl.ds(0, HALF)], s_z.at[g, 0, 0], r_r.at[g, zq, 0])
+            arrived(slot.at[pl.ds(HALF, HALF)], s_z.at[g, 0, 0], r_r.at[g, zq, 1])
             product(g, yo, zq)
             return carry
         lax.fori_loop(0, NZ, body, 0)
         far(acc.at[g, :, pl.ds(W, W + 128)], hr.at[g], s_h.at[g], r_h.at[g], twin).start()
 
     def hidden(g):
-        arrived(hr.at[g], s_z.at[g, 0], r_h.at[g])
+        arrived(hr.at[g], s_z.at[g, 0, 0], r_h.at[g])
         ss = acc[g, :, 2 * W:] + hr[g, :, W:]
         radius = jnp.sqrt(jnp.sum(ss, axis=-1, keepdims=True) / width + EPS)
         h = (acc[g, :, :W] + hr[g, :, :W]) / radius
@@ -255,102 +284,149 @@
         radius, h = hidden(g)
         outb[slot] = (xg[g, y, z].astype(F32) + gelu_value(h)).astype(BF)
 
-    own_sends(B, fwd_in.at[0])
-    far(stash_in.at[0, 0], xg.at[A, y, z], s_ev.at[0], r_ev.at[0], mirror).start()
-    near(fwd_in.at[0], xg.at[B, y, z], l_in.at[0]).start()
-    near(gain, gv, l_in.at[1]).start()
-    near(cot_in.at[0], cot.at[0], l_in.at[2]).start()
-    for k, yy in enumerate((y, yl, yr, yo)):
-        near(weight.at[:, yy, core], wc.at[yy, :, :, pl.ds(0, W)], l_w.at[k]).start()
-        far(weight.at[:, yy, 1 - core], wc.at[yy, :, :, pl.ds(W, W)], s_w.at[k], r_w.at[k], twin).start()
-    far(stash_in.at[0, 1], xg.at[C, y, z], s_ev.at[1], r_ev.at[1], mirror).start()
-    far(fwd_in.at[0], stash_out.at[0, 0], s_st.at[0], r_st.at[0], mirror).start()
-
-    @pl.when(sec == 0)
-    def _():
-        near(fresh_in, xg.at[D, y, z], l_in.at[3]).start()
-
-    @pl.when(sec == nsec - 1)
-    def _():
-        near(fresh_cot, cot.at[1], l_in.at[4]).start()
-
-    acc[...] = jnp.zeros_like(acc)
+    def mine(g):
+        return xg.at[g, y, z]
+
+    def weight_in():
+        for k, yy in enumerate((y, yl, yr, yo)):
+            far(weight.at[:, yy, 1 - core], wc.at[yy, :, :, pl.ds(W, W)], s_w.at[k], r_w.at[k], twin).start()
+
+    def small_in():
+        near(fwd_in.at[0], mine(B), l_in.at[0]).start()
+        near(gain, gv, l_in.at[1]).start()
+        near(cot_in.at[0], cot.at[0], l_in.at[2]).start()
+
+        @pl.when(sec == 0)
+        def _():
+            near(fresh_in, mine(D), l_in.at[3]).start()
+
+        @pl.when(sec == nsec - 1)
+        def _():
+            near(fresh_cot, cot.at[1], l_in.at[4]).start()
+
+        acc[...] = jnp.zeros_like(acc)
+
+    def small_wait():
+        near(fwd_in.at[0], mine(B), l_in.at[0]).wait()
+        near(gain, gv, l_in.at[1]).wait()
+        near(cot_in.at[0], cot.at[0], l_in.at[2]).wait()
+
+    def weight_wait():
+        for k, yy in enumerate((y, yl, yr, yo)):
+            near(weight.at[:, yy, core], wc.at[yy, :, :, pl.ds(0, W)], l_w.at[k]).wait()
+            arrived(wc.at[yy, :, :, pl.ds(W, W)], s_w.at[k], r_w.at[k])
+
+    def saved_in(b, g):
+        far(stash_in.at[0, b], mine(g), s_ev.at[b], r_ev.at[b], mirror).start()
+
+    def saved_wait(b, g):
+        arrived(mine(g), s_ev.at[b], r_ev.at[b])
+
+    def stash_first():
+        far(mine(B), stash_out.at[0, 0], s_st.at[0], r_st.at[0], mirror).start()
+
+    def stash_second():
+        far(mine(D), stash_out.at[0, 1], s_st.at[1], r_st.at[1], mirror).start()
+
+    def next_in():
+        @pl.when(sec < nsec - 1)
+        def _():
+            far(outb.at[0], mine(D), s_next, r_next, after).start()
+
+        near(outb.at[0], first_out.at[0], l_out.at[0]).start()
+
+    def next_wait():
+        @pl.when(sec == 0)
+        def _():
+            near(fresh_in, mine(D), l_in.at[3]).wait()
+
+        @pl.when(sec > 0)
+        def _():
+            arrived(mine(D), s_next, r_next)
+
+    def cot_out():
+        @pl.when(sec > 0)
+        def _():
+            far(outb.at[2], cot.at[1], s_prev, r_prev, before).start()
+
+        near(outb.at[2], first_grad.at[0], l_out.at[2]).start()
+
+    def cot_wait():
+        @pl.when(sec == nsec - 1)
+        def _():
+            near(fresh_cot, cot.at[1], l_in.at[4]).wait()
+
+        @pl.when(sec < nsec - 1)
+        def _():
+            arrived(cot.at[1], s_prev, r_prev)
+
+    def second_done():
+        near(outb.at[1], second_out.at[0], l_out.at[1]).start()
+
+    def grad_done():
+        near(outb.at[3], second_grad.at[0], l_out.at[3]).start()
+
+    saved_in(0, A)
+    own_up(B, fwd_in.at[0])
+    own_across(B, fwd_in.at[0])
+    weight_in()
+    small_in()
     column_sends(B)
-    near(fwd_in.at[0], xg.at[B, y, z], l_in.at[0]).wait()
-    near(gain, gv, l_in.at[1]).wait()
-    near(cot_in.at[0], cot.at[0], l_in.at[2]).wait()
-    arrived(xg.at[A, y, z], s_ev.at[0], r_ev.at[0])
-    own_sends(A, xg.at[A, y, z])
-    for k, yy in enumerate((y, yl, yr, yo)):
-        near(weight.at[:, yy, core], wc.at[yy, :, :, pl.ds(0, W)], l_w.at[k]).wait()
-        arrived(wc.at[yy, :, :, pl.ds(W, W)], s_w.at[k], r_w.at[k])
+    small_wait()
+    saved_wait(0, A)
+    own_up(A, mine(A))
+    own_across(A, mine(A))
+    saved_in(1, C)
+    weight_wait()
     relay(B)
     column_sends(A)
     last_quarter(B)
-    arrived(xg.at[C, y, z], s_ev.at[1], r_ev.at[1])
-    own_sends(C, xg.at[C, y, z])
     forward_end(B, 0)
-
-    @pl.when(sec < nsec - 1)
-    def _():
-        far(outb.at[0], xg.at[D, y, z], s_next, r_next, after).start()
-
-    near(outb.at[0], first_out.at[0], l_out.at[0]).start()
+    next_in()
     relay(A)
+    saved_wait(1, C)
+    own_up(C, mine(C))
+    last_quarter(A)
+    own_across(C, mine(C))
+    next_wait()
+    own_up(D, mine(D))
+    gradient_start(0, A)
+    scatter_over(0)
+    scatter_sides(0)
     column_sends(C)
-    last_quarter(A)
-
-    @pl.when(sec == 0)
-    def _():
-        near(fresh_in, xg.at[D, y, z], l_in.at[3]).wait()
-
-    @pl.when(sec > 0)
-    def _():
-        arrived(xg.at[D, y, z], s_next, r_next)
-
-    gradient_start(0, A)
+    stash_first()
+    scatter_column(0)
     relay(C)
-    scatter_over(0)
+    gradient_end(0, A)
+    cot_out()
     last_quarter(C)
-    scatter_sides(0)
-    own_sends(D, xg.at[D, y, z])
-    far(xg.at[D, y, z], stash_out.at[0, 1], s_st.at[1], r_st.at[1], mirror).start()
+    own_across(D, mine(D))
     column_sends(D)
-    scatter_column(0)
-    gradient_end(0, A)
-
-    @pl.when(sec > 0)
-    def _():
-        far(outb.at[2], cot.at[1], s_prev, r_prev, before).start()
-
-    near(outb.at[2], first_grad.at[0], l_out.at[2]).start()
-    relay(D)
-
-    @pl.when(sec == nsec - 1)
-    def _():
-        near(fresh_cot, cot.at[1], l_in.at[4]).wait()
-
-    @pl.when(sec < nsec - 1)
-    def _():
-        arrived(cot.at[1], s_prev, r_prev)
-
+    stash_second()
+    cot_wait()
     gradient_start(1, C)
     scatter_over(1)
+    relay(D)
+    scatter_sides(1)
     last_quarter(D)
-    scatter_sides(1)
+    scatter_column(1)
     forward_end(D, 1)
-    near(outb.at[1], second_out.at[0], l_out.at[1]).start()
-    scatter_column(1)
+    second_done()
     gradient_end(1, C)
-    near(outb.at[3], second_grad.at[0], l_out.at[3]).start()
+    grad_done()
 
     for g in range(4):
-        own = fwd_in.at[0] if g == B else xg.at[g, y, z]
-        for k in range(1, NZ):
-            sent(own, s_z.at[g, k], r_z.at[g, z])
-
         def sends_of(i, carry):
             slot = xg.at[g, 0, i]
+
+            @pl.when((i <= z) & (z < NZ - 1))
+            def _():
+                sent(slot, s_z.at[g, i, 0], r_z.at[g, i])
+
+            @pl.when((i >= z) & (z > 0))
+            def _():
+                sent(slot, s_z.at[g, i, 1], r_z.at[g, i])
+
             half = slot.at[pl.ds(0, HALF)]
             for k in range(2):
                 sent(slot, s_y.at[g, i, k], r_y.at[g, i, k])
@@ -389,6 +465,11 @@
 
     for k, out in enumerate((first_out, second_out, first_grad, second_grad)):
         near(outb.at[k], out.at[0], l_out.at[k]).wait()
+
+
+def hand_over(*refs):
+    for k in range(5):
+        refs[5 + k][...] = refs[k][...]
 
 
 def shards(nsec, fresh_in, fwd_in, fresh_cot, cot_in, stash_in, weight, gain):
@@ -418,7 +499,7 @@
         vm((2, NY, 8, 128), F32),
         vm((2, NZ, 8, 128), F32),
         vm((2, 2, 8, 128), F32),
-        dma((4, NZ)), dma((4, NZ)),
+        dma((4, NZ, 2)), dma((4, NZ)),
         dma((4, NZ, 2)), dma((4, NZ, 2)),
         dma((4, NZ, 2)), dma((4, NZ, 2)),
         dma((4,)), dma((4,)), dma((4,)),
@@ -430,7 +511,7 @@
         dma((2, 7)), dma((2, 7)),
     ]
     anywhere = pl.BlockSpec(memory_space=pl.ANY)
-    return pl.pallas_call(
+    outs = pl.pallas_call(
         functools.partial(kernel, nsec),
         out_shape=(block, block, block, block, jax.ShapeDtypeStruct((1, 2, TOK, W), BF)),
         in_specs=[anywhere] * 7,
@@ -441,6 +522,10 @@
         ),
         cost_estimate=pl.CostEstimate(flops=7_250_000_000, bytes_accessed=12_000_000, transcendentals=200_000),
     )(fresh_in, fwd_in, fresh_cot, cot_in, stash_in, weight, gain)
+    return pl.pallas_call(
+        hand_over,
+        out_shape=tuple(jax.ShapeDtypeStruct(o.shape, o.dtype) for o in outs),
+    )(*outs)
 
 
 def solution(mesh):

time: 136 us -> 113 us (0.83)
  Pallas kernels: 127 us -> 111 us
  local copies, waits for them, and re-layouts: 7.79 us -> 0 us
    pallas_call x1, Pallas kernels: 127 us -> 109 us  [shards(): pl.pallas_call(functools.partial(kernel, nsec), out_shape=(block, block,...]
    unnamed x5 -> x0, local copies, waits for them, and re-layouts: 7.79 us -> none
    pallas_call x0 -> x1, Pallas kernels: none -> 1.94 us  [shards(): pl.pallas_call(hand_over, out_shape=tuple((jax.ShapeDtypeStruct(o.shape,...]
where the time goes in v2:
time: 113 us; the launch traced here: 111 us
  Pallas kernels  111 us (98%)
    pallas_call x1, Pallas kernels, shards(): pl.pallas_call(functools.partial(kernel, nsec), out_shape=(block, block,...  109 us

profile of v2, /device:TPU:1, one launch (start us, length us, event | category | flops | bytes accessed | tf_op | source)
XLA Modules:
  0.0 111.3 jit_solution(11331596587938714852)
XLA Ops:
  0.6 108.8 %shard_map.110 = (bf16[1,128,384]{2,1,0:T(8,128)(2,1)}, bf16[1,128,384]{2,1,0:T(8,128)(2,1)}, bf16[1,128,384]{2,1,0:T(8,128)(2,1)}, bf16[1,128,384]{2,1,0:T(8,128)(2,1)}, bf16[1,2,128,384]{3,2,1,0:T(8,128)(2,1)}) custom-call(bf16[128,384]{1,0:T(8,128)(2,1)} %fresh_in.1, bf16[1,128,384]{2,1,0:T(8,128)(2,1)} %fwd_in.1, bf16[128,384]{1,0:T(8,128)(2,1)} %fresh_cot.1, ...), custom_call_target="tpu_custom_call" | custom-call | flops 7249999872 | bytes 12000000 | tf_op jit(solution)/shard_map/pallas_call | solution.py:514
  109.4 1.9 %shard_map.111 = (bf16[1,128,384]{2,1,0:T(8,128)(2,1)}, bf16[1,128,384]{2,1,0:T(8,128)(2,1)}, bf16[1,128,384]{2,1,0:T(8,128)(2,1)}, bf16[1,128,384]{2,1,0:T(8,128)(2,1)}, bf16[1,2,128,384]{3,2,1,0:T(8,128)(2,1)}) custom-call(bf16[1,128,384]{2,1,0:T(8,128)(2,1)} %get-tuple-element.10.refs_0_, bf16[1,128,384]{2,1,0:T(8,128)(2,1)} %get-tuple-element.11.refs_1_, ...), custom_call_target="tpu_custom_call" | custom-call | tf_op jit(solution)/shard_map/pallas_call | solution.py:525

commit v3 on v2

--- a/solution.py
+++ b/solution.py
@@ -17,6 +17,7 @@
 NY = 4
 HALF = TOK // 2
 A, B, C, D = 0, 1, 2, 3
+UNI = (A, C, D,)
 BF = jnp.bfloat16
 F32 = jnp.float32
 
@@ -81,6 +82,21 @@
     def near(src, dst, sem):
         return pltpu.make_async_copy(src, dst, sem)
 
+    def local_in():
+        near(fwd_in.at[0], xg.at[B, y, z], l_in.at[0]).start()
+        near(gain, gv, l_in.at[1]).start()
+        near(cot_in.at[0], cot.at[0], l_in.at[2]).start()
+
+        @pl.when(sec == 0)
+        def _():
+            near(fresh_in, xg.at[D, y, z], l_in.at[3]).start()
+
+        @pl.when(sec == nsec - 1)
+        def _():
+            near(fresh_cot, cot.at[1], l_in.at[4]).start()
+
+        acc[...] = jnp.zeros_like(acc)
+
     for k, yy in enumerate((y, yl, yr, yo)):
         near(weight.at[:, yy, core], wc.at[yy, :, :, pl.ds(0, W)], l_w.at[k]).start()
     barrier = pltpu.get_barrier_semaphore()
@@ -92,6 +108,7 @@
         greet(at(turn(z, k, NZ), y))
     for dev in (right, left, over, twin, mirror, after, before):
         greet(dev)
+    local_in()
     pl.semaphore_wait(barrier, 10)
 
     below, above = at(turn(z, 3, NZ), y), at(turn(z, 1, NZ), y)
@@ -107,6 +124,12 @@
         far(src, xg.at[g, y, zq], s_z.at[g, zq, 1], r_z.at[g, zq], below).start()
 
     def own_up(g, src):
+        if g in UNI:
+            for k in range(1, NZ):
+                far(src, xg.at[g, y, z], s_z.at[g, k, 0], r_z.at[g, z],
+                    at(turn(z, k, NZ), y)).start()
+            return
+
         @pl.when(z < NZ - 1)
         def _():
             go_up(g, src, z)
@@ -125,13 +148,14 @@
             slot = xg.at[g, y, zq]
             arrived(slot, s_z.at[g, 0, 0], r_z.at[g, zq])
 
-            @pl.when((zq < z) & (z < NZ - 1))
-            def _():
-                go_up(g, slot, zq)
-
-            @pl.when((zq > z) & (z > 0))
-            def _():
-                go_down(g, slot, zq)
+            if g not in UNI:
+                @pl.when((zq < z) & (z < NZ - 1))
+                def _():
+                    go_up(g, slot, zq)
+
+                @pl.when((zq > z) & (z > 0))
+                def _():
+                    go_down(g, slot, zq)
 
             far(slot, slot, s_y.at[g, zq, 0], r_y.at[g, zq, 0], right).start()
             far(slot, slot, s_y.at[g, zq, 1], r_y.at[g, zq, 1], left).start()
@@ -203,7 +227,7 @@
 
     def scatter_over(b):
         def body(i, carry):
-            zq = turn(z, i, NZ)
+            zq = nearest(NZ - i)
             hsend[b, zq] = part(b, yo, zq).astype(BF)
             far(hsend.at[b, zq, pl.ds(0, HALF)], hin.at[b, zq, pl.ds(0, HALF)],
                 s_a.at[b, zq, 0], r_a.at[b, zq, 0], right).start()
@@ -220,7 +244,7 @@
                 at(z, turn(y, k, NY))).start()
 
         def body(i, carry):
-            zq = turn(z, i, NZ)
+            zq = nearest(NZ - i)
             to_right = part(b, yr, zq)
             arrived(hin.at[b, zq, pl.ds(0, HALF)], s_a.at[b, zq, 0], r_a.at[b, zq, 0])
             fsend[b, zq, 0, :HALF] = (to_right[:HALF] + hin[b, zq, :HALF].astype(F32)).astype(BF)
@@ -251,7 +275,7 @@
                 at(turn(z, k, NZ), y)).start()
 
         def body(i, carry):
-            zq = turn(z, i, NZ)
+            zq = nearest(NZ - i)
             zsend[b, zq] = own_column(b, zq).astype(BF)
             far(zsend.at[b, zq], zin.at[b, z], s_c.at[b, zq], r_c.at[b, z], at(zq, y)).start()
             return carry
@@ -291,21 +315,6 @@
         for k, yy in enumerate((y, yl, yr, yo)):
             far(weight.at[:, yy, 1 - core], wc.at[yy, :, :, pl.ds(W, W)], s_w.at[k], r_w.at[k], twin).start()
 
-    def small_in():
-        near(fwd_in.at[0], mine(B), l_in.at[0]).start()
-        near(gain, gv, l_in.at[1]).start()
-        near(cot_in.at[0], cot.at[0], l_in.at[2]).start()
-
-        @pl.when(sec == 0)
-        def _():
-            near(fresh_in, mine(D), l_in.at[3]).start()
-
-        @pl.when(sec == nsec - 1)
-        def _():
-            near(fresh_cot, cot.at[1], l_in.at[4]).start()
-
-        acc[...] = jnp.zeros_like(acc)
-
     def small_wait():
         near(fwd_in.at[0], mine(B), l_in.at[0]).wait()
         near(gain, gv, l_in.at[1]).wait()
@@ -370,7 +379,6 @@
     own_up(B, fwd_in.at[0])
     own_across(B, fwd_in.at[0])
     weight_in()
-    small_in()
     column_sends(B)
     small_wait()
     saved_wait(0, A)
@@ -397,11 +405,11 @@
     stash_first()
     scatter_column(0)
     relay(C)
+    own_across(D, mine(D))
+    column_sends(D)
     gradient_end(0, A)
     cot_out()
     last_quarter(C)
-    own_across(D, mine(D))
-    column_sends(D)
     stash_second()
     cot_wait()
     gradient_start(1, C)
@@ -416,16 +424,21 @@
     grad_done()
 
     for g in range(4):
+        if g in UNI:
+            for k in range(1, NZ):
+                sent(xg.at[g, y, z], s_z.at[g, k, 0], r_z.at[g, z])
+
         def sends_of(i, carry):
             slot = xg.at[g, 0, i]
 
-            @pl.when((i <= z) & (z < NZ - 1))
-            def _():
-                sent(slot, s_z.at[g, i, 0], r_z.at[g, i])
-
-            @pl.when((i >= z) & (z > 0))
-            def _():
-                sent(slot, s_z.at[g, i, 1], r_z.at[g, i])
+            if g not in UNI:
+                @pl.when((i <= z) & (z < NZ - 1))
+                def _():
+                    sent(slot, s_z.at[g, i, 0], r_z.at[g, i])
+
+                @pl.when((i >= z) & (z > 0))
+                def _():
+                    sent(slot, s_z.at[g, i, 1], r_z.at[g, i])
 
             half = slot.at[pl.ds(0, HALF)]
             for k in range(2):

time: 113 us -> 110 us (0.973)
  Pallas kernels: 111 us -> 109 us
    pallas_call x1, Pallas kernels: 109 us -> 107 us  [shards(): pl.pallas_call(functools.partial(kernel, nsec), out_shape=(block, block,...]
where the time goes in v3:
time: 110 us; the launch traced here: 109 us
  Pallas kernels  109 us (99%)
    pallas_call x1, Pallas kernels, shards(): pl.pallas_call(functools.partial(kernel, nsec), out_shape=(block, block,...  107 us

profile of v3, /device:TPU:1, one launch (start us, length us, event | category | flops | bytes accessed | tf_op | source)
XLA Modules:
  0.0 109.4 jit_solution(5055758536763405955)
XLA Ops:
  0.6 106.8 %shard_map.110 = (bf16[1,128,384]{2,1,0:T(8,128)(2,1)}, bf16[1,128,384]{2,1,0:T(8,128)(2,1)}, bf16[1,128,384]{2,1,0:T(8,128)(2,1)}, bf16[1,128,384]{2,1,0:T(8,128)(2,1)}, bf16[1,2,128,384]{3,2,1,0:T(8,128)(2,1)}) custom-call(bf16[128,384]{1,0:T(8,128)(2,1)} %fresh_in.1, bf16[1,128,384]{2,1,0:T(8,128)(2,1)} %fwd_in.1, bf16[128,384]{1,0:T(8,128)(2,1)} %fresh_cot.1, ...), custom_call_target="tpu_custom_call" | custom-call | flops 7249999872 | bytes 12000000 | tf_op jit(solution)/shard_map/pallas_call | solution.py:527
  107.4 1.9 %shard_map.111 = (bf16[1,128,384]{2,1,0:T(8,128)(2,1)}, bf16[1,128,384]{2,1,0:T(8,128)(2,1)}, bf16[1,128,384]{2,1,0:T(8,128)(2,1)}, bf16[1,128,384]{2,1,0:T(8,128)(2,1)}, bf16[1,2,128,384]{3,2,1,0:T(8,128)(2,1)}) custom-call(bf16[1,128,384]{2,1,0:T(8,128)(2,1)} %get-tuple-element.10.refs_0_, bf16[1,128,384]{2,1,0:T(8,128)(2,1)} %get-tuple-element.11.refs_1_, ...), custom_call_target="tpu_custom_call" | custom-call | tf_op jit(solution)/shard_map/pallas_call | solution.py:538

commit v4 on v3

--- a/solution.py
+++ b/solution.py
@@ -320,8 +320,8 @@
         near(gain, gv, l_in.at[1]).wait()
         near(cot_in.at[0], cot.at[0], l_in.at[2]).wait()
 
-    def weight_wait():
-        for k, yy in enumerate((y, yl, yr, yo)):
+    def weight_wait(quarters):
+        for k, yy in quarters:
             near(weight.at[:, yy, core], wc.at[yy, :, :, pl.ds(0, W)], l_w.at[k]).wait()
             arrived(wc.at[yy, :, :, pl.ds(W, W)], s_w.at[k], r_w.at[k])
 
@@ -385,9 +385,10 @@
     own_up(A, mine(A))
     own_across(A, mine(A))
     saved_in(1, C)
-    weight_wait()
+    weight_wait(((0, y), (1, yl), (2, yr)))
     relay(B)
     column_sends(A)
+    weight_wait(((3, yo),))
     last_quarter(B)
     forward_end(B, 0)
     next_in()

time: 110 us -> 110 us (level)
  no operation moved by 1% of the time
where the time goes in v4:
time: 110 us; the launch traced here: 109 us
  Pallas kernels  109 us (99%)
    pallas_call x1, Pallas kernels, shards(): pl.pallas_call(functools.partial(kernel, nsec), out_shape=(block, block,...  107 us

profile of v4, /device:TPU:1, one launch (start us, length us, event | category | flops | bytes accessed | tf_op | source)
XLA Modules:
  0.0 109.4 jit_solution(10404857426117852884)
XLA Ops:
  0.6 106.8 %shard_map.110 = (bf16[1,128,384]{2,1,0:T(8,128)(2,1)}, bf16[1,128,384]{2,1,0:T(8,128)(2,1)}, bf16[1,128,384]{2,1,0:T(8,128)(2,1)}, bf16[1,128,384]{2,1,0:T(8,128)(2,1)}, bf16[1,2,128,384]{3,2,1,0:T(8,128)(2,1)}) custom-call(bf16[128,384]{1,0:T(8,128)(2,1)} %fresh_in.1, bf16[1,128,384]{2,1,0:T(8,128)(2,1)} %fwd_in.1, bf16[128,384]{1,0:T(8,128)(2,1)} %fresh_cot.1, ...), custom_call_target="tpu_custom_call" | custom-call | flops 7249999872 | bytes 12000000 | tf_op jit(solution)/shard_map/pallas_call | solution.py:528
  107.4 1.9 %shard_map.111 = (bf16[1,128,384]{2,1,0:T(8,128)(2,1)}, bf16[1,128,384]{2,1,0:T(8,128)(2,1)}, bf16[1,128,384]{2,1,0:T(8,128)(2,1)}, bf16[1,128,384]{2,1,0:T(8,128)(2,1)}, bf16[1,2,128,384]{3,2,1,0:T(8,128)(2,1)}) custom-call(bf16[1,128,384]{2,1,0:T(8,128)(2,1)} %get-tuple-element.10.refs_0_, bf16[1,128,384]{2,1,0:T(8,128)(2,1)} %get-tuple-element.11.refs_1_, ...), custom_call_target="tpu_custom_call" | custom-call | tf_op jit(solution)/shard_map/pallas_call | solution.py:539
